TPU v7x, 128 devices: a whole 4x4x4 slice. The times are simulated.
128 devices in a mesh: band: 32 (over x, z, core), dom: 4 (over y).
Axes of the slice: x: 4, y: 4, z: 4, core: 2. Of those that a mesh axis runs over, the one named last changes fastest.
Arguments:
- grid_inputs: bfloat16 [131072, 474], P(('band', 'dom')), may hold values from -6 to 6
- mesh_latent: bfloat16 [32768, 512], P(('band', 'dom')), may hold values from -6 to 6
- edge_state: bfloat16 [262144, 512], P(('band', 'dom')), may hold values from -6 to 6
- cotangent: bfloat16 [131072, 227], P(('band', 'dom')), may hold values from -0.15625 to 0.15625
- w_embed: bfloat16 [474, 512], replicated, may hold values from -0.25 to 0.25
- w_send: bfloat16 [512, 512], replicated, may hold values from -0.25 to 0.25
- w_recv: bfloat16 [512, 512], replicated, may hold values from -0.25 to 0.25
- w_edge: bfloat16 [1536, 512], replicated, may hold values from -0.15625 to 0.15625
- w_mesh_out: bfloat16 [512, 512], replicated, may hold values from -0.25 to 0.25
- w_grid_out: bfloat16 [512, 512], replicated, may hold values from -0.25 to 0.25
- w_predict: bfloat16 [512, 227], replicated, may hold values from -0.25 to 0.25
- enc_owner: int32 [131072, 1], P(('band', 'dom')), may hold values from 0 to 127; in each aligned block of 1024 rows (0 to 1023, 1024 to 2047, ...) at most 24 rows name the same one
- enc_local: int32 [131072], P(('band', 'dom')), may hold values from 0 to 255
- halo_rows: int32 [128, 128, 8], P(('band', 'dom')), may hold values from 0 to 255
- edge_src_dev: int32 [262144], P(('band', 'dom')), may hold values from 0 to 127
- edge_src_slot: int32 [262144], P(('band', 'dom')), may hold values from 0 to 7
- edge_dst: int32 [262144], P(('band', 'dom')), may hold values from 0 to 255
Outputs:
- prediction: bfloat16 [131072, 227], P(('band', 'dom'))
- grad_edge: float32 [1536, 512], P('band', 'dom')
Inputs may be any that keep to these rules, and one draw needn't show every extreme that they name: `enc_owner`: in the 1024 rows of one device no device index appears more than 24 times, and some index appears exactly 24 times.
All inputs are finite; a program needn't handle non-finite values.
Results may differ from a plain program's by a relative error of at most 0.015.
Values may be sent and summed in bfloat16 or wider, within the bound.
A program may use at most 128 MiB of HBM per device.

v0:
```python
import jax
import jax.numpy as jnp
from jax import lax
from jax.sharding import PartitionSpec as P


def swish(value):
    return value * jax.nn.sigmoid(value)


def norm_rows(values):
    center = values - jnp.mean(values, axis=-1, keepdims=True)
    spread = jnp.mean(center * center, axis=-1, keepdims=True)
    return center * lax.rsqrt(spread + 1e-05)


def body(
    grid_inputs,
    mesh_latent,
    edge_state,
    cotangent,
    w_embed,
    w_send,
    w_recv,
    w_edge,
    w_mesh_out,
    w_grid_out,
    w_predict,
    enc_owner,
    enc_local,
    halo_rows,
    edge_src_dev,
    edge_src_slot,
    edge_dst,
):
    shards = lax.axis_size(("band", "dom"))
    grid_count = grid_inputs.shape[0]
    nodes = mesh_latent.shape[0]
    width = w_send.shape[0]
    capacity = 3 * grid_count // shards
    halo_depth = halo_rows.shape[2]
    hidden = swish(jnp.dot(grid_inputs, w_embed, preferred_element_type=jnp.float32)).astype(
        jnp.bfloat16
    )
    owner = enc_owner[:, 0]
    member = (owner[:, None] == jnp.arange(shards, dtype=jnp.int32)[None, :]).astype(jnp.int32)
    rank = jnp.sum((jnp.cumsum(member, axis=0) - 1) * member, axis=1)
    slot = owner * capacity + rank
    buffer = jnp.zeros((shards * capacity, width), jnp.bfloat16).at[slot].set(hidden)
    labels = jnp.full((shards * capacity,), nodes, jnp.int32).at[slot].set(enc_local)
    got_rows, got_labels = (
        lax.all_to_all(
            buffer.reshape(shards, capacity, width),
            ("band", "dom"),
            split_axis=0,
            concat_axis=0,
            tiled=True,
        ),
        lax.all_to_all(
            labels.reshape(shards, capacity),
            ("band", "dom"),
            split_axis=0,
            concat_axis=0,
            tiled=True,
        ),
    )
    got_rows = got_rows.reshape(shards * capacity, width)
    got_labels = got_labels.reshape(shards * capacity)
    proj = jnp.dot(got_rows, w_send, preferred_element_type=jnp.float32).astype(jnp.bfloat16)
    query = jnp.dot(mesh_latent, w_recv, preferred_element_type=jnp.float32)
    message = swish(proj.astype(jnp.float32) + jnp.take(query, got_labels, axis=0, mode="clip"))
    agg = jax.ops.segment_sum(message, got_labels, nodes)
    encoded = (mesh_latent.astype(jnp.float32) + norm_rows(agg)).astype(jnp.bfloat16)
    outbound = jnp.take(encoded, halo_rows[0].reshape(-1), axis=0).reshape(
        shards, halo_depth, width
    )
    inbound = lax.all_to_all(
        outbound, ("band", "dom"), split_axis=0, concat_axis=0, tiled=True
    ).reshape(shards * halo_depth, width)
    senders = jnp.take(inbound, edge_src_dev * halo_depth + edge_src_slot, axis=0)
    receivers = jnp.take(encoded, edge_dst, axis=0)
    joined = jnp.concatenate([edge_state, senders, receivers], axis=1)
    pre = jnp.dot(joined, w_edge, preferred_element_type=jnp.float32)
    edge_sum = jax.ops.segment_sum(swish(pre), edge_dst, nodes)
    updated = (encoded.astype(jnp.float32) + norm_rows(edge_sum)).astype(jnp.bfloat16)
    returned = jnp.take(updated, got_labels, axis=0, mode="clip").reshape(shards, capacity, width)
    arrived = lax.all_to_all(
        returned, ("band", "dom"), split_axis=0, concat_axis=0, tiled=True
    ).reshape(shards * capacity, width)
    read = jnp.take(arrived, slot, axis=0)
    zed = jnp.dot(read, w_mesh_out, preferred_element_type=jnp.float32) + jnp.dot(
        hidden, w_grid_out, preferred_element_type=jnp.float32
    )
    act = swish(zed).astype(jnp.bfloat16)
    prediction = jnp.dot(act, w_predict, preferred_element_type=jnp.float32).astype(jnp.bfloat16)
    d_act = jnp.dot(cotangent, w_predict.T, preferred_element_type=jnp.float32)
    _, swish_back = jax.vjp(swish, zed)
    d_zed = swish_back(d_act)[0].astype(jnp.bfloat16)
    d_read = jnp.dot(d_zed, w_mesh_out.T, preferred_element_type=jnp.float32).astype(jnp.bfloat16)
    d_buffer = jnp.zeros((shards * capacity, width), jnp.bfloat16).at[slot].set(d_read)
    d_got = lax.all_to_all(
        d_buffer.reshape(shards, capacity, width),
        ("band", "dom"),
        split_axis=0,
        concat_axis=0,
        tiled=True,
    ).reshape(shards * capacity, width)
    d_updated = jax.ops.segment_sum(d_got.astype(jnp.float32), got_labels, nodes)
    _, norm_back = jax.vjp(norm_rows, edge_sum)
    d_sum = norm_back(d_updated)[0]
    d_edge = jnp.take(d_sum, edge_dst, axis=0)
    _, edge_back = jax.vjp(swish, pre)
    d_pre = edge_back(d_edge)[0].astype(jnp.bfloat16)
    partial_grad = lax.dot_general(
        joined, d_pre, (((0,), (0,)), ((), ())), preferred_element_type=jnp.float32
    )
    summed = lax.psum(partial_grad, ("band", "dom"))
    row_share = 3 * width // lax.axis_size("band")
    col_share = width // lax.axis_size("dom")
    grad_edge = lax.dynamic_slice(
        summed,
        (lax.axis_index("band") * row_share, lax.axis_index("dom") * col_share),
        (row_share, col_share),
    )
    return (prediction, grad_edge)


def solution(mesh):
    return jax.shard_map(
        body,
        mesh=mesh,
        in_specs=(
            P(("band", "dom"), None),
            P(("band", "dom"), None),
            P(("band", "dom"), None),
            P(("band", "dom"), None),
            P(),
            P(),
            P(),
            P(),
            P(),
            P(),
            P(),
            P(("band", "dom"), None),
            P(("band", "dom")),
            P(("band", "dom"), None, None),
            P(("band", "dom")),
            P(("band", "dom")),
            P(("band", "dom")),
        ),
        out_specs=(P(("band", "dom"), None), P("band", "dom")),
        check_vma=False,
    )
```

profile of v0, /device:TPU:1, one launch (start us, length us, event | category | flops | bytes accessed | tf_op | source)
XLA Modules:
  0.0 512.5 jit_solution(7959959813851605226)
XLA Ops:
  9.6 4.5 scatter_custom_fusion
  14.9 11.5 %all-to-all-start = ((s32[128,1,24]{2,1,0:T(1,128)}), s32[128,1,24]{2,1,0:T(1,128)S(1)}, u32[]{:S(2)}, u32[]{:S(2)}) async-start(s32[128,1,24]{2,1,0:T(1,128)} %bitcast.7), calls=%async_computation | async-start | bytes 131072 | tf_op jit(solution)/shard_map/all_to_all | solution.py:59
  26.4 3.2 fusion.54
  29.5 8.4 %scatter_custom_fusion.1 = bf16[3072,512]{1,0:T(8,128)(2,1)} fusion(s32[1024]{0:T(1024)S(1)} %bitcast.51, bf16[]{:T(256)} %constant.75.clone.1, f32[1024,512]{1,0:T(8,128)} %fusion.54), kind=kCustom, calls=%fused_computation.50 | custom fusion | flops 2621440 | bytes 5242882 | tf_op jit(solution)/shard_map/scatter | solution.py:49
  37.9 10.5 %all-to-all-start.1 = ((bf16[128,24,512]{2,1,0:T(8,128)(2,1)}), bf16[128,24,512]{2,1,0:T(8,128)(2,1)}, u32[]{:S(2)}, u32[]{:S(2)}) async-start(bf16[128,24,512]{2,1,0:T(8,128)(2,1)} %bitcast.44), calls=%async_computation.1 | async-start | bytes 6291456 | tf_op jit(solution)/shard_map/all_to_all | solution.py:52
  50.6 39.6 %all-to-all-done.1 = bf16[128,24,512]{2,1,0:T(8,128)(2,1)} async-done(((bf16[128,24,512]{2,1,0:T(8,128)(2,1)}), bf16[128,24,512]{2,1,0:T(8,128)(2,1)}, u32[]{:S(2)}, u32[]{:S(2)}) %all-to-all-start.1) | async-done | bytes 3145760 | tf_op jit(solution)/shard_map/all_to_all | solution.py:52
  90.2 5.5 %convolution_convert_fusion = bf16[3072,512]{1,0:T(8,128)(2,1)} fusion(bf16[3072,512]{1,0:T(8,128)(2,1)} %bitcast.9, bf16[512,512]{1,0:T(8,128)(2,1)} %param.22), kind=kOutput, calls=%fused_computation.25 | convolution fusion | flops 1612185600 | bytes 6815744 | tf_op jit(solution)/shard_map/dot_general | solution.py:69
  95.7 32.1 %scatter_custom_fusion.2 = f32[256,512]{1,0:T(8,128)S(1)} fusion(s32[3072]{0:T(1024)S(1)} %reshape.226, bf16[3072,512]{1,0:T(8,128)(2,1)} %convolution_convert_fusion, f32[]{:T(128)} %constant.76.clone.1, f32[]{:T(128)} %constant.73.clone.1, f32[256,512]{1,0:T(8,128)S(1)} %fusion.55, s32[3072]{0:T(1024)S(1)} %broadcast_clamp_fusion), kind=kCustom, calls=%fused_computation.17 | custom fusion | flops 11010048 | bytes 4206600 | tf_op jit(solution)/shard_map/scatter-add | solution.py:72
  128.3 4.0 gather_fusion
  133.5 4.1 all-to-all-start.2
  137.7 9.2 %gather_fusion.2 = bf16[2048,512]{1,0:T(8,128)(2,1)} fusion(bf16[256,512]{1,0:T(8,128)(2,1)S(1)} %add_convert_fusion.1, s32[2048]{0:T(1024)S(1)} %fusion.41), kind=kCustom, calls=%fused_computation.3 | custom fusion | bytes 4202496 | tf_op jit(solution)/shard_map/jit(_take)/gather | solution.py:81
  146.9 2.7 broadcast_select_fusion
  149.7 7.6 %all-to-all-done.2 = bf16[128,8,512]{2,1,0:T(8,128)(2,1)S(1)} async-done(((bf16[128,8,512]{2,1,0:T(8,128)(2,1)}), bf16[128,8,512]{2,1,0:T(8,128)(2,1)S(1)}, u32[]{:S(2)}, u32[]{:S(2)}) %all-to-all-start.2) | async-done | bytes 1048608 | tf_op jit(solution)/shard_map/all_to_all | solution.py:77
  157.3 9.2 %gather_fusion.1 = bf16[2048,512]{1,0:T(8,128)(2,1)} fusion(bf16[1024,512]{1,0:T(8,128)(2,1)S(1)} %bitcast.41, s32[2048]{0:T(1024)S(1)} %broadcast_clamp_fusion.1), kind=kCustom, calls=%fused_computation.2 | custom fusion | bytes 4202496 | tf_op jit(solution)/shard_map/jit(_take)/gather | solution.py:80
  166.5 1.9 broadcast_select_fusion.1
  168.4 1.4 copy-done.7
  169.8 4.9 fusion.17
  174.7 14.5 %scatter_custom_fusion.3 = f32[256,512]{1,0:T(8,128)S(1)} fusion(s32[2048]{0:T(1024)S(1)} %copy-done.15, f32[2048,512]{1,0:T(8,128)} %fusion.17, f32[]{:T(128)} %constant.76.clone.1, f32[]{:T(128)} %constant.73.clone.1), kind=kCustom, calls=%fused_computation.29 | custom fusion | flops 5242880 | bytes 4718600 | tf_op jit(solution)/shard_map/scatter-add | solution.py:84
  189.7 13.2 %gather_fusion.3 = bf16[3072,512]{1,0:T(8,128)(2,1)} fusion(bf16[256,512]{1,0:T(8,128)(2,1)S(1)} %add_convert_fusion, s32[3072]{0:T(1024)S(1)} %broadcast_clamp_fusion), kind=kCustom, calls=%fused_computation.4 | custom fusion | bytes 6303744 | tf_op jit(solution)/shard_map/jit(_take)/gather | solution.py:86
  202.9 3.7 all-to-all-start.3
  206.7 42.3 %all-to-all-done.3 = bf16[128,24,512]{2,1,0:T(8,128)(2,1)S(1)} async-done(((bf16[128,24,512]{2,1,0:T(8,128)(2,1)}), bf16[128,24,512]{2,1,0:T(8,128)(2,1)S(1)}, u32[]{:S(2)}, u32[]{:S(2)}) %all-to-all-start.3) | async-done | bytes 3145760 | tf_op jit(solution)/shard_map/all_to_all | solution.py:87
  249.0 5.1 gather_fusion.4
  254.1 2.3 fusion.29
  256.4 2.0 convolution_add_fusion
  258.4 3.9 convolution_convert_fusion.1
  262.3 6.9 %scatter_custom_fusion.4 = bf16[3072,512]{1,0:T(8,128)(2,1)S(1)} fusion(s32[1024]{0:T(1024)S(1)} %bitcast.53, bf16[1024,512]{1,0:T(8,128)(2,1)} %convolution_convert_fusion.1, bf16[]{:T(256)} %constant.75.clone.1), kind=kCustom, calls=%fused_computation.48 | custom fusion | bytes 3146240 | tf_op jit(solution)/shard_map/scatter | solution.py:100
  269.3 46.1 %all_to_all.29 = bf16[128,24,512]{2,1,0:T(8,128)(2,1)} all-to-all(bf16[128,24,512]{2,1,0:T(8,128)(2,1)S(1)} %bitcast.43), channel_id=1, replica_groups=mesh['band'=32,'dom'=4] {'band','dom'}, dimensions={0} | all-to-all | bytes 6291456 | tf_op jit(solution)/shard_map/all_to_all | solution.py:101
  315.3 19.6 %scatter_custom_fusion.5 = f32[256,512]{1,0:T(8,128)S(1)} fusion(s32[3072]{0:T(1024)S(1)} %reshape.226, bf16[3072,512]{1,0:T(8,128)(2,1)} %bitcast.45, f32[]{:T(128)} %constant.73.clone.1), kind=kCustom, calls=%fused_computation.14 | custom fusion | flops 3145728 | bytes 3670020 | tf_op jit(solution)/shard_map/scatter-add | solution.py:108
  335.6 8.9 %gather_fusion.5 = f32[2048,512]{1,0:T(8,128)} fusion(f32[256,512]{1,0:T(8,128)S(1)} %broadcast_add_fusion, s32[2048]{0:T(1024)S(1)} %fusion.41), kind=kCustom, calls=%fused_computation.6 | custom fusion | bytes 8396800 | tf_op jit(solution)/shard_map/jit(_take)/gather | solution.py:111
  344.5 10.5 %fusion.16 = f32[1536,512]{1,0:T(8,128)} fusion(bf16[2048,512]{1,0:T(8,128)(2,1)S(1)} %copy-done.6, bf16[2048,512]{1,0:T(8,128)(2,1)} %copy-done.7, bf16[2048,512]{1,0:T(8,128)(2,1)} %param.19, f32[2048,512]{1,0:T(8,128)} %fusion.17, f32[2048,512]{1,0:T(8,128)} %gather_fusion.5, pred[2048]{0:T(1024)(128)(4,1)S(1)} %compare_and_fusion), kind=kOutput, calls=%fused_computation.34 | convolution fusion | flops 3251634176 | bytes 17827840 | tf_op jit(solution)/shard_map/dot_general | solution.py:114
  355.0 3.3 convolution_convert_fusion.2
  358.3 145.5 %all-reduce.2.cloned.1.call-done = f32[1536,512]{1,0:T(8,128)} async-done(((f32[1536,512]{1,0:T(8,128)}), f32[1536,512]{1,0:T(8,128)}) %all-reduce.2.cloned.1.call-update) | async-done | bytes 3145744 | tf_op jit(solution)/shard_map/psum | solution.py:117
  (87 shorter events, 9.5 us)
Async XLA Ops:
  7.2 162.6 %copy-start = (bf16[1536,512]{1,0:T(8,128)(2,1)S(1)}, bf16[1536,512]{1,0:T(8,128)(2,1)}, u32[]{:S(2)}) copy-start(bf16[1536,512]{1,0:T(8,128)(2,1)} %param.24) | copy-start | bytes 4718596
  7.2 2.4 copy-start.12
  7.2 19.2 %copy-start.9 = (bf16[1024,474]{0,1:T(8,128)(2,1)S(1)}, bf16[1024,474]{0,1:T(8,128)(2,1)}, u32[]{:S(2)}) copy-start(bf16[1024,474]{0,1:T(8,128)(2,1)} %param.17) | copy-start | bytes 2912260
  14.9 23.1 %all-to-all-start = ((s32[128,1,24]{2,1,0:T(1,128)}), s32[128,1,24]{2,1,0:T(1,128)S(1)}, u32[]{:S(2)}, u32[]{:S(2)}) async-start(s32[128,1,24]{2,1,0:T(1,128)} %bitcast.7), calls=%async_computation | async-start | bytes 131072 | tf_op jit(solution)/shard_map/all_to_all | solution.py:59
  37.9 10.6 %copy-start.16 = (s32[1,128,8]{1,2,0:T(8,128)S(1)}, s32[1,128,8]{1,2,0:T(8,128)}, u32[]{:S(2)}) copy-start(s32[1,128,8]{1,2,0:T(8,128)} %param.30) | copy-start | bytes 12292
  37.9 10.9 %copy-start.15 = (s32[2048]{0:T(1024)S(1)}, s32[2048]{0:T(1024)}, u32[]{:S(2)}) copy-start(s32[2048]{0:T(1024)} %param.33) | copy-start | bytes 24580
  37.9 10.9 %copy-start.8 = (bf16[256,512]{1,0:T(8,128)(2,1)S(1)}, bf16[256,512]{1,0:T(8,128)(2,1)}, u32[]{:S(2)}) copy-start(bf16[256,512]{1,0:T(8,128)(2,1)} %param.18) | copy-start | bytes 786436
  37.9 10.9 %copy-start.10 = (bf16[512,512]{1,0:T(8,128)(2,1)S(1)}, bf16[512,512]{1,0:T(8,128)(2,1)}, u32[]{:S(2)}) copy-start(bf16[512,512]{1,0:T(8,128)(2,1)} %param.23) | copy-start | bytes 1572868
  37.9 52.3 %all-to-all-start.1 = ((bf16[128,24,512]{2,1,0:T(8,128)(2,1)}), bf16[128,24,512]{2,1,0:T(8,128)(2,1)}, u32[]{:S(2)}, u32[]{:S(2)}) async-start(bf16[128,24,512]{2,1,0:T(8,128)(2,1)} %bitcast.44), calls=%async_computation.1 | async-start | bytes 6291456 | tf_op jit(solution)/shard_map/all_to_all | solution.py:52
  132.3 5.4 %copy-start.13 = (s32[2048]{0:T(1024)S(1)}, s32[2048]{0:T(1024)}, u32[]{:S(2)}) copy-start(s32[2048]{0:T(1024)} %param.32) | copy-start | bytes 24580
  132.3 5.4 %copy-start.14 = (s32[2048]{0:T(1024)S(1)}, s32[2048]{0:T(1024)}, u32[]{:S(2)}) copy-start(s32[2048]{0:T(1024)} %param.31) | copy-start | bytes 24580
  133.5 23.8 %all-to-all-start.2 = ((bf16[128,8,512]{2,1,0:T(8,128)(2,1)}), bf16[128,8,512]{2,1,0:T(8,128)(2,1)S(1)}, u32[]{:S(2)}, u32[]{:S(2)}) async-start(bf16[128,8,512]{2,1,0:T(8,128)(2,1)} %bitcast_select_fusion), calls=%async_computation.2 | async-start | bytes 2097152 | tf_op jit(solution)/shard_map/all_to_all | solution.py:77
  166.5 3.4 copy-start.5
  166.5 3.4 copy-start.17
  168.4 1.4 copy-start.7
  189.2 13.8 %copy-start.2 = (f32[256,512]{1,0:T(8,128)}, f32[256,512]{1,0:T(8,128)S(1)}, u32[]{:S(2)}) copy-start(f32[256,512]{1,0:T(8,128)S(1)} %scatter_custom_fusion.3) | copy-start | bytes 1572868
  202.9 46.1 %all-to-all-start.3 = ((bf16[128,24,512]{2,1,0:T(8,128)(2,1)}), bf16[128,24,512]{2,1,0:T(8,128)(2,1)S(1)}, u32[]{:S(2)}, u32[]{:S(2)}) async-start(bf16[128,24,512]{2,1,0:T(8,128)(2,1)} %bitcast.46), calls=%async_computation.3 | async-start | bytes 6291456 | tf_op jit(solution)/shard_map/all_to_all | solution.py:87
  206.6 297.2 %all-reduce.2.cloned.1.call-start = ((), (), s32[]{:S(2)}) async-start(), calls=%async_computation.5 | async-start | bytes 6291456 | tf_op jit(solution)/shard_map/psum | solution.py:117
  254.1 2.3 copy-start.4
  254.1 2.3 copy-start.18
  256.3 2.1 copy-start.11
  256.4 2.1 copy-start.19
  256.4 2.1 copy-start.20
  315.3 19.6 %copy-start.3 = (f32[256,512]{1,0:T(8,128)S(1)}, f32[256,512]{1,0:T(8,128)}, u32[]{:S(2)}) copy-start(f32[256,512]{1,0:T(8,128)} %copy-done.2) | copy-start | bytes 1572868
  335.6 8.9 %copy-start.6 = (bf16[2048,512]{1,0:T(8,128)(2,1)S(1)}, bf16[2048,512]{1,0:T(8,128)(2,1)}, u32[]{:S(2)}) copy-start(bf16[2048,512]{1,0:T(8,128)(2,1)} %broadcast_select_fusion) | copy-start | bytes 6291460
  355.0 150.2 %copy-start.1 = (bf16[1536,512]{1,0:T(8,128)(2,1)S(1)}, bf16[1536,512]{1,0:T(8,128)(2,1)}, u32[]{:S(2)}) copy-start(bf16[1536,512]{1,0:T(8,128)(2,1)} %param.24) | copy-start | bytes 4718596
Sparse Core Ops, SparseCore 0:
  355.1 148.6 all-reduce.1
where the time goes:
time: 519 us; the launch traced here: 512 us
  waiting for transfers between devices  235 us (45%)
  other arithmetic  84.2 us (16%)
  local copies, waits for them, and re-layouts  66.5 us (13%)
  blocking collectives  46.1 us (9%)
  matrix products  35.8 us (7%)
  starting transfers between devices  29.9 us (6%)
  between operations  15 us (3%)
    psum x1, waiting for transfers between devices, body(): summed = lax.psum(partial_grad, ('band', 'dom'))  146 us
    all_to_all x1, blocking collectives, body(): lax.all_to_all(d_buffer.reshape(shards, capacity, width), ('band', 'dom')...  46.1 us
    all_to_all x1, waiting for transfers between devices, body(): lax.all_to_all(returned, ('band', 'dom'), split_axis=0, concat_axis=0, ti...  42.3 us
    all_to_all x1, waiting for transfers between devices, body(): lax.all_to_all(buffer.reshape(shards, capacity, width), ('band', 'dom'),...  39.6 us
    scatter-add x1, other arithmetic, body(): agg = jax.ops.segment_sum(message, got_labels, nodes)  32.1 us
    scatter-add x1, other arithmetic, body(): jax.ops.segment_sum(d_got.astype(jnp.float32), got_labels, nodes)  19.6 us
    scatter-add x1, other arithmetic, body(): edge_sum = jax.ops.segment_sum(swish(pre), edge_dst, nodes)  14.5 us
    gather x1, local copies, waits for them, and re-layouts, body(): jnp.take(updated, got_labels, axis=0, mode='clip')  13.2 us
  transfers between devices with their start and end apart: 5, of which 4 were waited for; matrix products, arithmetic and copies ran while one was open for 6% of the time, Pallas kernels for 0%

commit v1 on v0

v1 whole, which is shorter than its diff:
```python
import functools

import jax
import jax.numpy as jnp
from jax import lax
from jax.experimental import pallas as pl
from jax.experimental.pallas import tpu as pltpu
from jax.sharding import PartitionSpec as P

MESH = pl.DeviceIdType.MESH
F32 = jnp.float32
BF16 = jnp.bfloat16
CHUNKS = 8
STRIDE = 53
STRIDE_INVERSE = 29


def sigmoid(value):
    return 0.5 * jnp.tanh(0.5 * value) + 0.5


def dot(a, b):
    return jnp.dot(a, b, preferred_element_type=F32)


def one_hot(mask):
    return jnp.where(mask, 1.0, 0.0).astype(BF16)


def iota(shape, dim):
    return lax.broadcasted_iota(jnp.int32, shape, dim)


def column(row):
    wide = jnp.broadcast_to(row.astype(F32), (8, row.shape[1]))
    return jnp.transpose(wide)[:, :1].astype(jnp.int32)


def moments(values):
    center = values - jnp.mean(values, axis=-1, keepdims=True)
    spread = jnp.mean(center * center, axis=-1, keepdims=True)
    scale = lax.rsqrt(spread + 1e-05)
    return center * scale, scale


def fold(values, parts, depth):
    half = values.shape[1] // 2
    cut = values.reshape(parts, depth, 2 * half)
    return jnp.concatenate([cut[:, :, :half], cut[:, :, half:]], axis=1).astype(BF16)


def unfold(values):
    parts, twice, half = values.shape
    depth = twice // 2
    wide = values.astype(F32)
    return jnp.concatenate([wide[:, :depth], wide[:, depth:]], axis=2).reshape(parts * depth, 2 * half)


def kernel(
    nx,
    nz,
    ny,
    cap,
    halo,
    x_ref,
    ml_ref,
    es_ref,
    cot_ref,
    wemb_ref,
    wsend_ref,
    wrecv_ref,
    wedge_ref,
    wm_ref,
    wg_ref,
    wp_ref,
    owner_ref,
    local_ref,
    halo_ref,
    dev_ref,
    slot_ref,
    dst_ref,
    pred_ref,
    grad_ref,
    xs,
    cs,
    web,
    wpp,
    wpt,
    slots,
    sbuf,
    rbuf,
    csbuf,
    crbuf,
    obuf,
    inbuf,
    bsend,
    bland,
    hbuf,
    own,
    ownt,
    query,
    agg,
    enc,
    hal,
    osnd,
    orcv,
    orcvt,
    part,
    est,
    inb,
    snd,
    esum,
    mesh_part,
    dz,
    dsum,
    dpre,
    gland,
    g2,
    gl2,
    pick,
    a_send,
    a_recv,
    c_send,
    c_recv,
    h_send,
    h_recv,
    b_send,
    b_recv,
    p_send,
    p_recv,
    g_send,
    g_recv,
):
    n = nx * nz * 2 * ny
    chips = nx * nz * ny
    grid, width_in = x_ref.shape
    nodes, width = ml_ref.shape
    edges = es_ref.shape[0]
    outs = cot_ref.shape[1]
    spc = n // CHUNKS
    rows = spc * cap
    epc = edges // CHUNKS
    band, y = lax.axis_index("band"), lax.axis_index("dom")
    x, z, k = band // (2 * nz), (band // 2) % nz, band % 2
    me = band * ny + y

    def shift(r, sign):
        q = (r * STRIDE) % n
        dy, dk, dz_, dx = q % ny, (q // ny) % 2, (q // (2 * ny)) % nz, q // (2 * ny * nz)
        tx = (x + sign * dx + nx) % nx
        tz = (z + sign * dz_ + nz) % nz
        tk = (k + dk) % 2
        ty = (y + sign * dy + ny) % ny
        return (tx * nz + tz) * 2 + tk, ty

    barrier = pltpu.get_barrier_semaphore()

    def greet(r, carry):
        tb, ty = shift(r, 1)
        pl.semaphore_signal(barrier, inc=1, device_id=(tb, ty), device_id_type=MESH)
        return carry

    lax.fori_loop(1, n, greet, 0)

    o = owner_ref[...]
    member = jnp.where(o == iota((n, grid), 0), 1.0, 0.0)
    tri = min(128, grid)
    before = one_hot(iota((tri, tri), 0) < iota((tri, tri), 1))
    base = jnp.zeros((n, 1), F32)
    ranks = []
    for i in range(grid // tri):
        m = member[:, i * tri : (i + 1) * tri]
        count = dot(m.astype(BF16), before) + base
        ranks.append(jnp.sum(count * m, axis=0, keepdims=True))
        base = base + jnp.sum(m, axis=1, keepdims=True)
    rank = jnp.concatenate(ranks, axis=1).astype(jnp.int32)
    ly, lz = ny.bit_length() - 1, nz.bit_length() - 1
    qy = ((o & (ny - 1)) - y) & (ny - 1)
    qk = ((o >> ly) - k) & 1
    qz = ((o >> (ly + 1)) - z) & (nz - 1)
    qx = ((o >> (ly + 1 + lz)) - x) & (nx - 1)
    q = ((qx * nz + qz) * 2 + qk) * ny + qy
    slots[...] = ((q * STRIDE_INVERSE) & (n - 1)) * cap + rank

    xs[...] = jnp.zeros_like(xs)
    xs[:, :width_in] = x_ref[...]
    tail = xs[:, width - 128 :].astype(F32)
    mark = iota((grid, 128), 1) == width_in - (width - 128)
    xs[:, width - 128 :] = jnp.where(mark, (column(local_ref[...]) + 1).astype(F32), tail).astype(BF16)
    cs[...] = jnp.zeros_like(cs)
    cs[:, :outs] = cot_ref[...]

    pl.semaphore_wait(barrier, n - 1)

    def send(src, dst, send_sem, recv_sem, to):
        pltpu.make_async_remote_copy(
            src_ref=src, dst_ref=dst, send_sem=send_sem, recv_sem=recv_sem, device_id=to, device_id_type=MESH
        ).start()

    def take(ref, sem):
        pltpu.make_async_copy(ref, ref, sem).wait()

    def send_parts(c, src, dst, send_sem, recv_sem, sign):
        def one(i, carry):
            r = c * spc + i

            @pl.when(r > 0)
            def _():
                send(src.at[r], dst.at[r], send_sem, recv_sem.at[c], shift(r, sign))

            return carry

        lax.fori_loop(0, spc, one, 0)

        @pl.when(c == 0)
        def _():
            pltpu.make_async_copy(src.at[0], dst.at[0], recv_sem.at[0]).start()

    def pack(c, carry):
        place = one_hot(slots[...] == iota((rows, grid), 0) + c * rows)
        sbuf[pl.ds(c * spc, spc)] = fold(dot(place, xs[...]), spc, cap)
        send_parts(c, sbuf, rbuf, a_send, a_recv, 1)
        csbuf[pl.ds(c * spc, spc)] = fold(dot(place, cs[...]), spc, cap)
        return carry

    lax.fori_loop(0, CHUNKS, pack, 0)

    web[...] = jnp.zeros_like(web)
    web[:width_in, :] = wemb_ref[...]
    wpp[...] = jnp.zeros_like(wpp)
    wpp[:, :outs] = wp_ref[...]
    wpt[...] = jnp.transpose(wpp[...])
    query[...] = dot(ml_ref[...], wrecv_ref[...]).astype(BF16)

    def encode(c, carry):
        take(rbuf.at[pl.ds(c * spc, spc)], a_recv.at[c])
        wide = unfold(rbuf[pl.ds(c * spc, spc)])
        mark = iota((rows, 128), 1) == width_in - (width - 128)
        label = jnp.sum(jnp.where(mark, wide[:, width - 128 :], 0.0), axis=1, keepdims=True)
        hit = one_hot(label.astype(jnp.int32) - 1 == iota((rows, nodes), 1))
        lines = pl.ds(pl.multiple_of(c * rows, rows), rows)
        own[lines, :] = hit
        hit_t = jnp.transpose(hit)
        ownt[:, lines] = hit_t
        hid = dot(wide.astype(BF16), web[...])
        hid = (hid * sigmoid(hid)).astype(BF16)
        hbuf[lines, :] = hid
        arg = dot(hid, wsend_ref[...]) + dot(hit, query[...])
        agg[...] += dot(hit_t, (arg * sigmoid(arg)).astype(BF16))
        return carry

    def prepare(c, carry):
        lines = pl.ds(pl.multiple_of(c * epc, epc), epc)
        dst = dst_ref[:, lines]
        orcvt[:, lines] = one_hot(dst == iota((nodes, epc), 0))
        orcv[lines, :] = one_hot(column(dst) == iota((epc, nodes), 1))
        source = column(dev_ref[:, lines] * halo + slot_ref[:, lines])
        osnd[lines, :] = one_hot(source == iota((epc, n * halo), 1))
        state = es_ref[lines, :]
        est[:, lines] = jnp.transpose(state)
        part[lines, :] = dot(state, wedge_ref[:width, :])
        hpc = n * halo // CHUNKS
        spots = pl.ds(pl.multiple_of(c * hpc, hpc), hpc)
        hal[spots, :] = one_hot(column(halo_ref[:, spots]) == iota((hpc, nodes), 1))
        gpc = grid // CHUNKS
        spots = pl.ds(pl.multiple_of(c * gpc, gpc), gpc)
        pick[spots, :] = one_hot(column(slots[:, spots]) == iota((gpc, n * cap), 1))
        return carry

    lax.fori_loop(0, CHUNKS, prepare, 0)
    agg[...] = jnp.zeros_like(agg)
    lax.fori_loop(0, CHUNKS, encode, 0)

    encoded = (ml_ref[...].astype(F32) + moments(agg[...])[0]).astype(BF16)
    enc[...] = encoded

    def outbound(c, carry):
        hpc = n * halo // CHUNKS
        spots = pl.ds(pl.multiple_of(c * hpc, hpc), hpc)
        obuf[pl.ds(c * spc, spc)] = fold(dot(hal[spots, :], enc[...]), spc, halo)
        return carry

    lax.fori_loop(0, CHUNKS, outbound, 0)

    def send_halo(r, carry):
        tb, ty = shift(r, 1)
        send(obuf.at[tb * ny + ty], inbuf.at[me], h_send, h_recv, (tb, ty))
        return carry

    lax.fori_loop(1, n, send_halo, 0)
    pltpu.make_async_copy(obuf.at[me], inbuf.at[me], h_recv).start()

    def send_cot(c, carry):
        send_parts(c, csbuf, crbuf, c_send, c_recv, 1)
        return carry

    lax.fori_loop(0, CHUNKS, send_cot, 0)

    own_part = dot(enc[...], wedge_ref[2 * width :, :]).astype(BF16)
    mesh_part[...] = own_part

    def edge_own(c, carry):
        lines = pl.ds(pl.multiple_of(c * epc, epc), epc)
        part[lines, :] += dot(orcv[lines, :], mesh_part[...])
        return carry

    lax.fori_loop(0, CHUNKS, edge_own, 0)
    esum[...] = jnp.zeros_like(esum)
    take(inbuf, h_recv)
    inb[...] = unfold(inbuf[...]).astype(BF16)

    def edge_forward(c, carry):
        lines = pl.ds(pl.multiple_of(c * epc, epc), epc)
        sender = dot(osnd[lines, :], inb[...]).astype(BF16)
        snd[lines, :] = sender
        pre = part[lines, :] + dot(sender, wedge_ref[width : 2 * width, :])
        part[lines, :] = pre
        esum[...] += dot(orcvt[:, lines], (pre * sigmoid(pre)).astype(BF16))
        return carry

    lax.fori_loop(0, CHUNKS, edge_forward, 0)
    normed, scale = moments(esum[...])
    updated = (enc[...].astype(F32) + normed).astype(BF16)
    mesh_part[...] = dot(updated, wm_ref[...]).astype(BF16)
    dz[...] = jnp.zeros_like(dz)

    def decode(c, carry):
        lines = pl.ds(pl.multiple_of(c * rows, rows), rows)
        zed = dot(hbuf[lines, :], wg_ref[...]) + dot(own[lines, :], mesh_part[...])
        sig = sigmoid(zed)
        bsend[pl.ds(c * spc, spc)] = fold(dot((zed * sig).astype(BF16), wpp[...]), spc, cap)

        def one(i, inner):
            r = c * spc + i

            @pl.when(r > 0)
            def _():
                send(bsend.at[r], bland.at[r], b_send, b_recv, shift(r, -1))

            return inner

        lax.fori_loop(0, spc, one, 0)
        take(crbuf.at[pl.ds(c * spc, spc)], c_recv.at[c])
        slope = dot(unfold(crbuf[pl.ds(c * spc, spc)]).astype(BF16), wpt[...])
        slope = (slope * sig * (1.0 + zed * (1.0 - sig))).astype(BF16)
        dz[...] += dot(ownt[:, lines], slope)
        return carry

    lax.fori_loop(0, CHUNKS, decode, 0)
    pltpu.make_async_copy(bsend.at[0], bland.at[0], b_recv).start()

    slope = lax.dot_general(
        dz[...].astype(BF16), wm_ref[...], (((1,), (1,)), ((), ())), preferred_element_type=F32
    )
    normed, scale = moments(esum[...])
    slope = scale * (
        slope
        - jnp.mean(slope, axis=-1, keepdims=True)
        - normed * jnp.mean(slope * normed, axis=-1, keepdims=True)
    )
    dsum[...] = slope.astype(BF16)

    def edge_backward(c, carry):
        lines = pl.ds(pl.multiple_of(c * epc, epc), epc)
        pre = part[lines, :]
        sig = sigmoid(pre)
        slope = dot(orcv[lines, :], dsum[...])
        dpre[lines, :] = (slope * sig * (1.0 + pre * (1.0 - sig))).astype(BF16)
        return carry

    lax.fori_loop(0, CHUNKS, edge_backward, 0)
    hbuf[:width, :] = dot(est[...], dpre[...]).astype(BF16)
    hbuf[width : 2 * width, :] = lax.dot_general(
        snd[...], dpre[...], (((0,), (0,)), ((), ())), preferred_element_type=F32
    ).astype(BF16)
    received = dot(orcvt[...], dpre[...]).astype(BF16)
    hbuf[2 * width : 3 * width, :] = lax.dot_general(
        enc[...], received, (((0,), (0,)), ((), ())), preferred_element_type=F32
    ).astype(BF16)

    share = 3 * width // (nx * nz * 2)

    def send_pair(i, carry):
        block = pl.ds(pl.multiple_of((i * 2 + 1 - k) * share, 16), share)
        send(hbuf.at[block, :], gland.at[i], p_send, p_recv, ((x * nz + z) * 2 + 1 - k, y))
        return carry

    lax.fori_loop(0, nx * nz, send_pair, 0)
    take(gland, p_recv)
    cols = width // ny

    def add_pair(i, carry):
        block = pl.ds(pl.multiple_of((i * 2 + k) * share, 16), share)
        both = (hbuf[block, :].astype(F32) + gland[i].astype(F32)).astype(BF16)
        for d in range(ny):
            g2[i * ny + d] = both[:, d * cols : (d + 1) * cols]
        return carry

    lax.fori_loop(0, nx * nz, add_pair, 0)
    chip = (x * nz + z) * ny + y

    def send_grad(r, carry):
        q = (r * STRIDE) % chips
        ty = (y + q % ny) % ny
        tz = (z + (q // ny) % nz) % nz
        tx = (x + q // (ny * nz)) % nx
        xz = tx * nz + tz
        send(g2.at[xz * ny + ty], gl2.at[chip], g_send, g_recv, (xz * 2 + k, ty))
        return carry

    lax.fori_loop(1, chips, send_grad, 0)
    pltpu.make_async_copy(g2.at[chip], gl2.at[chip], g_recv).start()

    take(bland, b_recv)

    def arrange(c, carry):
        lines = pl.ds(pl.multiple_of(c * rows, rows), rows)
        own[lines, :] = unfold(bland[pl.ds(c * spc, spc)]).astype(BF16)
        return carry

    lax.fori_loop(0, CHUNKS, arrange, 0)

    def choose(c, carry):
        gpc = grid // CHUNKS
        spots = pl.ds(pl.multiple_of(c * gpc, gpc), gpc)
        pred_ref[spots, :] = dot(pick[spots, :], own[...])[:, :outs].astype(BF16)
        return carry

    lax.fori_loop(0, CHUNKS, choose, 0)
    take(gl2, g_recv)
    grad_ref[...] = jnp.zeros_like(grad_ref)

    def add_grad(i, carry):
        grad_ref[...] += gl2[i].astype(F32)
        return carry

    lax.fori_loop(0, chips, add_grad, 0)
    take(sbuf.at[pl.ds(1, n - 1)], a_send)
    take(csbuf.at[pl.ds(1, n - 1)], c_send)
    take(obuf.at[pl.ds(1, n - 1)], h_send)
    take(bsend.at[pl.ds(1, n - 1)], b_send)
    take(gland, p_send)
    take(g2.at[pl.ds(1, chips - 1)], g_send)


def body(
    grid_inputs,
    mesh_latent,
    edge_state,
    cotangent,
    w_embed,
    w_send,
    w_recv,
    w_edge,
    w_mesh_out,
    w_grid_out,
    w_predict,
    enc_owner,
    enc_local,
    halo_rows,
    edge_src_dev,
    edge_src_slot,
    edge_dst,
    bands,
    doms,
):
    side = int(round((bands // 2) ** 0.5))
    n = bands * doms
    chips = n // 2
    grid = grid_inputs.shape[0]
    nodes, width = mesh_latent.shape
    edges = edge_state.shape[0]
    outs = cotangent.shape[1]
    wide_out = 256
    cap = 3 * grid // n
    halo = halo_rows.shape[2]
    share, cols = 3 * width // bands, width // doms
    vmem = pltpu.VMEM
    scratch = [
        vmem((grid, width), BF16),
        vmem((grid, wide_out), BF16),
        vmem((width, width), BF16),
        vmem((width, wide_out), BF16),
        vmem((wide_out, width), BF16),
        vmem((1, grid), jnp.int32),
        vmem((n, 2 * cap, width // 2), BF16),
        vmem((n, 2 * cap, width // 2), BF16),
        vmem((n, 2 * cap, wide_out // 2), BF16),
        vmem((n, 2 * cap, wide_out // 2), BF16),
        vmem((n, 2 * halo, width // 2), BF16),
        vmem((n, 2 * halo, width // 2), BF16),
        vmem((n, 2 * cap, wide_out // 2), BF16),
        vmem((n, 2 * cap, wide_out // 2), BF16),
        vmem((max(n * cap, 3 * width), width), BF16),
        vmem((n * cap, nodes), BF16),
        vmem((nodes, n * cap), BF16),
        vmem((nodes, width), BF16),
        vmem((nodes, width), F32),
        vmem((nodes, width), BF16),
        vmem((n * halo, nodes), BF16),
        vmem((edges, n * halo), BF16),
        vmem((edges, nodes), BF16),
        vmem((nodes, edges), BF16),
        vmem((edges, width), F32),
        vmem((width, edges), BF16),
        vmem((n * halo, width), BF16),
        vmem((edges, width), BF16),
        vmem((nodes, width), F32),
        vmem((nodes, width), BF16),
        vmem((nodes, width), F32),
        vmem((nodes, width), BF16),
        vmem((edges, width), BF16),
        vmem((bands // 2, share, width), BF16),
        vmem((chips, share, cols), BF16),
        vmem((chips, share, cols), BF16),
        vmem((grid, n * cap), BF16),
    ]
    dma = pltpu.SemaphoreType.DMA
    for _ in range(2):
        scratch += [dma, dma((CHUNKS,))]
    scratch += [dma] * 8
    return pl.pallas_call(
        functools.partial(kernel, side, side, doms, cap, halo),
        out_shape=(
            jax.ShapeDtypeStruct((grid, outs), BF16),
            jax.ShapeDtypeStruct((share, cols), F32),
        ),
        in_specs=[pl.BlockSpec(memory_space=vmem)] * 17,
        out_specs=(pl.BlockSpec(memory_space=vmem),) * 2,
        scratch_shapes=scratch,
        compiler_params=pltpu.CompilerParams(
            collective_id=0, has_side_effects=True, vmem_limit_bytes=63 * 1024 * 1024
        ),
        cost_estimate=pl.CostEstimate(flops=25 * 10**9, bytes_accessed=10**7, transcendentals=10**7),
    )(
        grid_inputs,
        mesh_latent,
        edge_state,
        cotangent,
        w_embed,
        w_send,
        w_recv,
        w_edge,
        w_mesh_out,
        w_grid_out,
        w_predict,
        enc_owner.reshape(1, grid),
        enc_local.reshape(1, grid),
        halo_rows.reshape(1, n * halo),
        edge_src_dev.reshape(1, edges),
        edge_src_slot.reshape(1, edges),
        edge_dst.reshape(1, edges),
    )


def solution(mesh):
    both = ("band", "dom")
    return jax.shard_map(
        functools.partial(body, bands=mesh.shape["band"], doms=mesh.shape["dom"]),
        mesh=mesh,
        in_specs=(P(both, None),) * 4
        + (P(),) * 7
        + (P(both, None), P(both), P(both, None, None), P(both), P(both), P(both)),
        out_specs=(P(both, None), P("band", "dom")),
        check_vma=False,
    )
```

time: 519 us -> 141 us (0.27)
  waiting for transfers between devices: 235 us -> 0 us
  Pallas kernels: 0 us -> 129 us
  other arithmetic: 84.2 us -> 0 us
  local copies, waits for them, and re-layouts: 66.5 us -> 10.1 us
  blocking collectives: 46.1 us -> 0 us
  matrix products: 35.8 us -> 0 us
  starting transfers between devices: 29.9 us -> 0 us
  between operations: 15 us -> 0.65 us
    psum x1 -> x0, waiting for transfers between devices: 146 us -> none  [body(): summed = lax.psum(partial_grad, ('band', 'dom'))]
    pallas_call x0 -> x1, Pallas kernels: none -> 129 us  [body(): pl.pallas_call(functools.partial(kernel, side, side, doms, cap, halo), ou...]
    all_to_all x4 -> x0, waiting for transfers between devices: 89.5 us -> none  [the longest x1 42.3 us: body(): lax.all_to_all(returned, ('band', 'dom'), split_axis=0, concat_axis=0, ti...]
    scatter-add x3 -> x0, other arithmetic: 66.2 us -> none  [the longest x1 32.1 us: body(): agg = jax.ops.segment_sum(message, got_labels, nodes)]
    gather x6 -> x0, local copies, waits for them, and re-layouts: 49.5 us -> none  [the longest x1 13.2 us: body(): jnp.take(updated, got_labels, axis=0, mode='clip')]
    all_to_all x1 -> x0, blocking collectives: 46.1 us -> none  [body(): lax.all_to_all(d_buffer.reshape(shards, capacity, width), ('band', 'dom')...]
    dot_general x9 -> x0, matrix products: 35.8 us -> none  [the longest x1 10.5 us: body(): lax.dot_general(joined, d_pre, (((0,), (0,)), ((), ())), preferred_elemen...]
    all_to_all x4 -> x0, starting transfers between devices: 29.9 us -> none  [the longest x1 11.5 us: body(): lax.all_to_all(labels.reshape(shards, capacity), ('band', 'dom'), split_a...]
  transfers between devices with their start and end apart: 5 -> 0, of which waited for: 4 -> 0; matrix products, arithmetic and copies ran while one was open for 6% -> 0% of each run, Pallas kernels for 0% -> 0%
where the time goes in v1:
time: 141 us; the launch traced here: 139 us
  Pallas kernels  129 us (91%)
  local copies, waits for them, and re-layouts  10.1 us (7%)
    pallas_call x1, Pallas kernels, body(): pl.pallas_call(functools.partial(kernel, side, side, doms, cap, halo), ou...  129 us
    unnamed x7, local copies, waits for them, and re-layouts  7.35 us

profile of v1, /device:TPU:1, one launch (start us, length us, event | category | flops | bytes accessed | tf_op | source)
XLA Modules:
  0.0 139.4 jit_solution(17531490594286016192)
XLA Ops:
  0.6 0.0 copy-start
  0.6 0.9 copy.24
  1.5 0.7 reshape.24.halo_ref
  2.2 1.8 %copy.27.wp_ref = bf16[512,227]{1,0:T(8,128)(2,1)} copy(bf16[512,227]{0,1:T(8,128)(2,1)} %param.27) | data formatting | bytes 464896 | tf_op args[10]
  4.0 2.0 %copy.26.cot_ref = bf16[1024,227]{1,0:T(8,128)(2,1)} copy(bf16[1024,227]{0,1:T(8,128)(2,1)} %param.20) | data formatting | bytes 929792 | tf_op args[3]
  6.0 0.0 copy-done
  6.0 1.3 copy.25.x_ref
  7.3 128.7 %shard_map.176 = (bf16[1024,227]{1,0:T(8,128)(2,1)}, f32[48,128]{1,0:T(8,128)}) custom-call(bf16[1024,474]{1,0:T(8,128)(2,1)} %copy.25.x_ref, bf16[256,512]{1,0:T(8,128)(2,1)} %ml_ref.1, bf16[2048,512]{1,0:T(8,128)(2,1)} %es_ref.1, bf16[1024,227]{1,0:T(8,128)(2,1)} %copy.26.cot_ref, bf16[474,512]{1,0:T(8,128)(2,1)} %wemb_ref.1, bf16[512,512]{1,0:T(8,128)(2,1)} %wsend_ref.1, ...), custom_call_target="tpu_custom_call" | custom-call | flops 24999999488 | bytes 10000000 | tf_op jit(solution)/shard_map/pallas_call | solution.py:522
  136.1 2.0 %copy.28 = bf16[1024,227]{0,1:T(8,128)(2,1)} copy(bf16[1024,227]{1,0:T(8,128)(2,1)} %get-tuple-element.4) | data formatting | bytes 929792 | tf_op jit(solution)/shard_map/pallas_call | solution.py:522
  138.1 1.3 copy.30
Async XLA Ops:
  0.6 5.4 %copy-start = (bf16[1024,474]{0,1:T(8,128)(2,1)S(1)}, bf16[1024,474]{0,1:T(8,128)(2,1)}, u32[]{:S(2)}) copy-start(bf16[1024,474]{0,1:T(8,128)(2,1)} %param.17) | copy-start | bytes 2912260

commit v2 on v1

--- a/solution.py
+++ b/solution.py
@@ -11,6 +11,8 @@
 F32 = jnp.float32
 BF16 = jnp.bfloat16
 CHUNKS = 8
+EARLY = 2
+INPUTS = 17
 STRIDE = 53
 STRIDE_INVERSE = 29
 
@@ -21,6 +23,10 @@
 
 def dot(a, b):
     return jnp.dot(a, b, preferred_element_type=F32)
+
+
+def dot_t(a, b):
+    return lax.dot_general(a, b, (((1,), (1,)), ((), ())), preferred_element_type=F32)
 
 
 def one_hot(mask):
@@ -62,106 +68,115 @@
     ny,
     cap,
     halo,
-    x_ref,
-    ml_ref,
-    es_ref,
-    cot_ref,
-    wemb_ref,
-    wsend_ref,
-    wrecv_ref,
-    wedge_ref,
-    wm_ref,
-    wg_ref,
-    wp_ref,
-    owner_ref,
-    local_ref,
-    halo_ref,
-    dev_ref,
-    slot_ref,
-    dst_ref,
-    pred_ref,
-    grad_ref,
-    xs,
-    cs,
-    web,
-    wpp,
-    wpt,
-    slots,
-    sbuf,
-    rbuf,
-    csbuf,
-    crbuf,
-    obuf,
-    inbuf,
-    bsend,
-    bland,
-    hbuf,
-    own,
-    ownt,
-    query,
-    agg,
-    enc,
-    hal,
-    osnd,
-    orcv,
-    orcvt,
-    part,
-    est,
-    inb,
-    snd,
-    esum,
-    mesh_part,
-    dz,
-    dsum,
-    dpre,
-    gland,
-    g2,
-    gl2,
-    pick,
-    a_send,
-    a_recv,
-    c_send,
-    c_recv,
-    h_send,
-    h_recv,
-    b_send,
-    b_recv,
-    p_send,
-    p_recv,
-    g_send,
-    g_recv,
+    *refs,
 ):
+    inputs, refs = refs[:INPUTS], refs[INPUTS:]
+    pred_ref, grad_ref, *refs = refs
+    held, loaded, refs = refs[:INPUTS], refs[INPUTS], refs[INPUTS + 1 :]
+    (
+        x_ref,
+        ml_ref,
+        es_ref,
+        cot_ref,
+        wemb_ref,
+        wsend_ref,
+        wrecv_ref,
+        wedge_ref,
+        wm_ref,
+        wg_ref,
+        wp_ref,
+        owner_ref,
+        local_ref,
+        halo_ref,
+        dev_ref,
+        slot_ref,
+        dst_ref,
+    ) = held
+    (
+        xs,
+        cs,
+        web,
+        wpp,
+        wpt,
+        slots,
+        sbuf,
+        rbuf,
+        csbuf,
+        crbuf,
+        obuf,
+        inbuf,
+        bsend,
+        bland,
+        hbuf,
+        own,
+        ownt,
+        query,
+        agg,
+        enc,
+        hal,
+        osnd,
+        orcv,
+        orcvt,
+        part,
+        est,
+        inb,
+        snd,
+        esum,
+        mesh_part,
+        dz,
+        dsum,
+        dpre,
+        gland,
+        g2,
+        gl2,
+        pick,
+        a_send,
+        a_recv,
+        c_send,
+        c_recv,
+        h_send,
+        h_recv,
+        b_send,
+        b_recv,
+        p_send,
+        p_recv,
+        g_send,
+        g_recv,
+    ) = refs
     n = nx * nz * 2 * ny
     chips = nx * nz * ny
-    grid, width_in = x_ref.shape
+    width_in, grid = x_ref.shape
     nodes, width = ml_ref.shape
     edges = es_ref.shape[0]
-    outs = cot_ref.shape[1]
+    outs = cot_ref.shape[0]
     spc = n // CHUNKS
     rows = spc * cap
     epc = edges // CHUNKS
     band, y = lax.axis_index("band"), lax.axis_index("dom")
-    x, z, k = band // (2 * nz), (band // 2) % nz, band % 2
+    k = lax.rem(band, 2)
     me = band * ny + y
 
     def shift(r, sign):
-        q = (r * STRIDE) % n
-        dy, dk, dz_, dx = q % ny, (q // ny) % 2, (q // (2 * ny)) % nz, q // (2 * ny * nz)
-        tx = (x + sign * dx + nx) % nx
-        tz = (z + sign * dz_ + nz) % nz
-        tk = (k + dk) % 2
-        ty = (y + sign * dy + ny) % ny
-        return (tx * nz + tz) * 2 + tk, ty
+        to = lax.rem(me + r * (STRIDE if sign > 0 else n - STRIDE % n), n)
+        return lax.div(to, ny), lax.rem(to, ny)
 
     barrier = pltpu.get_barrier_semaphore()
 
     def greet(r, carry):
-        tb, ty = shift(r, 1)
-        pl.semaphore_signal(barrier, inc=1, device_id=(tb, ty), device_id_type=MESH)
+        pl.semaphore_signal(barrier, inc=1, device_id=shift(r, 1), device_id_type=MESH)
         return carry
 
     lax.fori_loop(1, n, greet, 0)
 
+    order = (11, 12, 0, 3, 1, 4, 6, 16, 14, 15, 2, 7, 13, 10, 5, 9, 8)
+    for i in order:
+        pltpu.make_async_copy(inputs[i], held[i], loaded.at[i]).start()
+
+    def ready(*which):
+        for i in which:
+            pltpu.make_async_copy(inputs[i], held[i], loaded.at[i]).wait()
+
+    ready(11, 12)
     o = owner_ref[...]
     member = jnp.where(o == iota((n, grid), 0), 1.0, 0.0)
     tri = min(128, grid)
@@ -174,21 +189,18 @@
         ranks.append(jnp.sum(count * m, axis=0, keepdims=True))
         base = base + jnp.sum(m, axis=1, keepdims=True)
     rank = jnp.concatenate(ranks, axis=1).astype(jnp.int32)
-    ly, lz = ny.bit_length() - 1, nz.bit_length() - 1
-    qy = ((o & (ny - 1)) - y) & (ny - 1)
-    qk = ((o >> ly) - k) & 1
-    qz = ((o >> (ly + 1)) - z) & (nz - 1)
-    qx = ((o >> (ly + 1 + lz)) - x) & (nx - 1)
-    q = ((qx * nz + qz) * 2 + qk) * ny + qy
-    slots[...] = ((q * STRIDE_INVERSE) & (n - 1)) * cap + rank
-
-    xs[...] = jnp.zeros_like(xs)
-    xs[:, :width_in] = x_ref[...]
-    tail = xs[:, width - 128 :].astype(F32)
-    mark = iota((grid, 128), 1) == width_in - (width - 128)
-    xs[:, width - 128 :] = jnp.where(mark, (column(local_ref[...]) + 1).astype(F32), tail).astype(BF16)
-    cs[...] = jnp.zeros_like(cs)
-    cs[:, :outs] = cot_ref[...]
+    slots[...] = (((o - me) * STRIDE_INVERSE) & (n - 1)) * cap + rank
+
+    ready(0, 3)
+    first = width_in // 16 * 16
+    xs[first:, :] = jnp.zeros((width - first, grid), BF16)
+    xs[:width_in, :] = x_ref[...]
+    tail = xs[first : first + 16, :].astype(F32)
+    mark = iota((16, grid), 0) == width_in - first
+    xs[first : first + 16, :] = jnp.where(mark, (local_ref[...] + 1).astype(F32), tail).astype(BF16)
+    first = outs // 16 * 16
+    cs[first:, :] = jnp.zeros((cs.shape[0] - first, grid), BF16)
+    cs[:outs, :] = cot_ref[...]
 
     pl.semaphore_wait(barrier, n - 1)
 
@@ -218,22 +230,36 @@
 
     def pack(c, carry):
         place = one_hot(slots[...] == iota((rows, grid), 0) + c * rows)
-        sbuf[pl.ds(c * spc, spc)] = fold(dot(place, xs[...]), spc, cap)
+        pick[pl.ds(pl.multiple_of(c * rows, rows), rows), :] = place
+        sbuf[pl.ds(c * spc, spc)] = fold(dot_t(place, xs[...]), spc, cap)
         send_parts(c, sbuf, rbuf, a_send, a_recv, 1)
-        csbuf[pl.ds(c * spc, spc)] = fold(dot(place, cs[...]), spc, cap)
+        csbuf[pl.ds(c * spc, spc)] = fold(dot_t(place, cs[...]), spc, cap)
         return carry
 
     lax.fori_loop(0, CHUNKS, pack, 0)
 
-    web[...] = jnp.zeros_like(web)
+    def send_cot(c, carry):
+        send_parts(c, csbuf, crbuf, c_send, c_recv, 1)
+        return carry
+
+    ready(1, 4, 6, 16, 14, 15, 2, 7, 13, 10, 5, 9, 8)
+    first = width_in // 16 * 16
+    web[first:, :] = jnp.zeros((width - first, width), BF16)
     web[:width_in, :] = wemb_ref[...]
-    wpp[...] = jnp.zeros_like(wpp)
-    wpp[:, :outs] = wp_ref[...]
-    wpt[...] = jnp.transpose(wpp[...])
+    first = outs // 16 * 16
+    wpt[first:, :] = jnp.zeros((wpt.shape[0] - first, width), BF16)
+    wpt[:outs, :] = wp_ref[...]
+    wpp[...] = jnp.transpose(wpt[...])
+    halo_col = jnp.transpose(halo_ref[...].astype(F32)).astype(BF16)
     query[...] = dot(ml_ref[...], wrecv_ref[...]).astype(BF16)
 
     def encode(c, carry):
         take(rbuf.at[pl.ds(c * spc, spc)], a_recv.at[c])
+
+        @pl.when(c == CHUNKS - 1)
+        def _():
+            lax.fori_loop(0, EARLY, send_cot, 0)
+
         wide = unfold(rbuf[pl.ds(c * spc, spc)])
         mark = iota((rows, 128), 1) == width_in - (width - 128)
         label = jnp.sum(jnp.where(mark, wide[:, width - 128 :], 0.0), axis=1, keepdims=True)
@@ -261,10 +287,11 @@
         part[lines, :] = dot(state, wedge_ref[:width, :])
         hpc = n * halo // CHUNKS
         spots = pl.ds(pl.multiple_of(c * hpc, hpc), hpc)
-        hal[spots, :] = one_hot(column(halo_ref[:, spots]) == iota((hpc, nodes), 1))
-        gpc = grid // CHUNKS
-        spots = pl.ds(pl.multiple_of(c * gpc, gpc), gpc)
-        pick[spots, :] = one_hot(column(slots[:, spots]) == iota((gpc, n * cap), 1))
+        to = (me + (iota((hpc, n), 0) + c * hpc) // halo * STRIDE) & (n - 1)
+        spread = one_hot(to == iota((hpc, n), 1))
+        label = jnp.where(iota((hpc, halo), 0) % halo == iota((hpc, halo), 1), dot(spread, halo_col), 0.0)
+        label = jnp.sum(label, axis=1, keepdims=True).astype(jnp.int32)
+        hal[spots, :] = one_hot(label == iota((hpc, nodes), 1))
         return carry
 
     lax.fori_loop(0, CHUNKS, prepare, 0)
@@ -278,23 +305,22 @@
         hpc = n * halo // CHUNKS
         spots = pl.ds(pl.multiple_of(c * hpc, hpc), hpc)
         obuf[pl.ds(c * spc, spc)] = fold(dot(hal[spots, :], enc[...]), spc, halo)
+
+        def one(i, inner):
+            r = c * spc + i
+
+            @pl.when(r > 0)
+            def _():
+                send(obuf.at[r], inbuf.at[me], h_send, h_recv, shift(r, 1))
+
+            return inner
+
+        lax.fori_loop(0, spc, one, 0)
         return carry
 
     lax.fori_loop(0, CHUNKS, outbound, 0)
-
-    def send_halo(r, carry):
-        tb, ty = shift(r, 1)
-        send(obuf.at[tb * ny + ty], inbuf.at[me], h_send, h_recv, (tb, ty))
-        return carry
-
-    lax.fori_loop(1, n, send_halo, 0)
-    pltpu.make_async_copy(obuf.at[me], inbuf.at[me], h_recv).start()
-
-    def send_cot(c, carry):
-        send_parts(c, csbuf, crbuf, c_send, c_recv, 1)
-        return carry
-
-    lax.fori_loop(0, CHUNKS, send_cot, 0)
+    pltpu.make_async_copy(obuf.at[0], inbuf.at[me], h_recv).start()
+    lax.fori_loop(EARLY, CHUNKS, send_cot, 0)
 
     own_part = dot(enc[...], wedge_ref[2 * width :, :]).astype(BF16)
     mesh_part[...] = own_part
@@ -369,23 +395,26 @@
         return carry
 
     lax.fori_loop(0, CHUNKS, edge_backward, 0)
+    share = 3 * width // (nx * nz * 2)
+
+    def send_pair(i, carry):
+        block = pl.ds(pl.multiple_of((i * 2 + 1 - k) * share, 16), share)
+        send(hbuf.at[block, :], gland.at[i], p_send, p_recv, (band + 1 - 2 * k, y))
+        return carry
+
     hbuf[:width, :] = dot(est[...], dpre[...]).astype(BF16)
+    cut = width // (2 * share)
+    lax.fori_loop(0, cut, send_pair, 0)
     hbuf[width : 2 * width, :] = lax.dot_general(
         snd[...], dpre[...], (((0,), (0,)), ((), ())), preferred_element_type=F32
     ).astype(BF16)
+    cut, done = 2 * width // (2 * share), cut
+    lax.fori_loop(done, cut, send_pair, 0)
     received = dot(orcvt[...], dpre[...]).astype(BF16)
     hbuf[2 * width : 3 * width, :] = lax.dot_general(
         enc[...], received, (((0,), (0,)), ((), ())), preferred_element_type=F32
     ).astype(BF16)
-
-    share = 3 * width // (nx * nz * 2)
-
-    def send_pair(i, carry):
-        block = pl.ds(pl.multiple_of((i * 2 + 1 - k) * share, 16), share)
-        send(hbuf.at[block, :], gland.at[i], p_send, p_recv, ((x * nz + z) * 2 + 1 - k, y))
-        return carry
-
-    lax.fori_loop(0, nx * nz, send_pair, 0)
+    lax.fori_loop(cut, nx * nz, send_pair, 0)
     take(gland, p_recv)
     cols = width // ny
 
@@ -397,15 +426,12 @@
         return carry
 
     lax.fori_loop(0, nx * nz, add_pair, 0)
-    chip = (x * nz + z) * ny + y
+    chip = lax.div(band, 2) * ny + y
 
     def send_grad(r, carry):
-        q = (r * STRIDE) % chips
-        ty = (y + q % ny) % ny
-        tz = (z + (q // ny) % nz) % nz
-        tx = (x + q // (ny * nz)) % nx
-        xz = tx * nz + tz
-        send(g2.at[xz * ny + ty], gl2.at[chip], g_send, g_recv, (xz * 2 + k, ty))
+        to = lax.rem(chip + r * STRIDE, chips)
+        xz = lax.div(to, ny)
+        send(g2.at[to], gl2.at[chip], g_send, g_recv, (xz * 2 + k, lax.rem(to, ny)))
         return carry
 
     lax.fori_loop(1, chips, send_grad, 0)
@@ -415,18 +441,18 @@
 
     def arrange(c, carry):
         lines = pl.ds(pl.multiple_of(c * rows, rows), rows)
-        own[lines, :] = unfold(bland[pl.ds(c * spc, spc)]).astype(BF16)
+        ownt[:, lines] = jnp.transpose(unfold(bland[pl.ds(c * spc, spc)]).astype(BF16))
         return carry
 
     lax.fori_loop(0, CHUNKS, arrange, 0)
+    gpc = min(256, grid)
 
     def choose(c, carry):
-        gpc = grid // CHUNKS
         spots = pl.ds(pl.multiple_of(c * gpc, gpc), gpc)
-        pred_ref[spots, :] = dot(pick[spots, :], own[...])[:, :outs].astype(BF16)
-        return carry
-
-    lax.fori_loop(0, CHUNKS, choose, 0)
+        pred_ref[:, spots] = dot(ownt[...], pick[:, spots])[:outs].astype(BF16)
+        return carry
+
+    lax.fori_loop(0, grid // gpc, choose, 0)
     take(gl2, g_recv)
     grad_ref[...] = jnp.zeros_like(grad_ref)
 
@@ -477,8 +503,8 @@
     share, cols = 3 * width // bands, width // doms
     vmem = pltpu.VMEM
     scratch = [
-        vmem((grid, width), BF16),
-        vmem((grid, wide_out), BF16),
+        vmem((width, grid), BF16),
+        vmem((wide_out, grid), BF16),
         vmem((width, width), BF16),
         vmem((width, wide_out), BF16),
         vmem((wide_out, width), BF16),
@@ -513,44 +539,47 @@
         vmem((bands // 2, share, width), BF16),
         vmem((chips, share, cols), BF16),
         vmem((chips, share, cols), BF16),
-        vmem((grid, n * cap), BF16),
+        vmem((n * cap, grid), BF16),
     ]
     dma = pltpu.SemaphoreType.DMA
     for _ in range(2):
         scratch += [dma, dma((CHUNKS,))]
     scratch += [dma] * 8
-    return pl.pallas_call(
+    operands = (
+        grid_inputs.T,
+        mesh_latent,
+        edge_state,
+        cotangent.T,
+        w_embed,
+        w_send,
+        w_recv,
+        w_edge,
+        w_mesh_out,
+        w_grid_out,
+        w_predict.T,
+        enc_owner.reshape(1, grid),
+        enc_local.reshape(1, grid),
+        halo_rows[0].T,
+        edge_src_dev.reshape(1, edges),
+        edge_src_slot.reshape(1, edges),
+        edge_dst.reshape(1, edges),
+    )
+    scratch = [vmem(a.shape, a.dtype) for a in operands] + [pltpu.SemaphoreType.DMA((INPUTS,))] + scratch
+    prediction, gradient = pl.pallas_call(
         functools.partial(kernel, side, side, doms, cap, halo),
         out_shape=(
-            jax.ShapeDtypeStruct((grid, outs), BF16),
+            jax.ShapeDtypeStruct((outs, grid), BF16),
             jax.ShapeDtypeStruct((share, cols), F32),
         ),
-        in_specs=[pl.BlockSpec(memory_space=vmem)] * 17,
+        in_specs=[pl.BlockSpec(memory_space=pl.ANY)] * INPUTS,
         out_specs=(pl.BlockSpec(memory_space=vmem),) * 2,
         scratch_shapes=scratch,
         compiler_params=pltpu.CompilerParams(
             collective_id=0, has_side_effects=True, vmem_limit_bytes=63 * 1024 * 1024
         ),
         cost_estimate=pl.CostEstimate(flops=25 * 10**9, bytes_accessed=10**7, transcendentals=10**7),
-    )(
-        grid_inputs,
-        mesh_latent,
-        edge_state,
-        cotangent,
-        w_embed,
-        w_send,
-        w_recv,
-        w_edge,
-        w_mesh_out,
-        w_grid_out,
-        w_predict,
-        enc_owner.reshape(1, grid),
-        enc_local.reshape(1, grid),
-        halo_rows.reshape(1, n * halo),
-        edge_src_dev.reshape(1, edges),
-        edge_src_slot.reshape(1, edges),
-        edge_dst.reshape(1, edges),
-    )
+    )(*operands)
+    return prediction.T, gradient
 
 
 def solution(mesh):

time: 141 us -> 125 us (0.89)
  Pallas kernels: 129 us -> 119 us
  local copies, waits for them, and re-layouts: 10.1 us -> 3.17 us
    pallas_call x1, Pallas kernels: 129 us -> 119 us  [body(): pl.pallas_call(functools.partial(kernel, side, side, doms, cap, halo), ou...]
    unnamed x7 -> x2, local copies, waits for them, and re-layouts: 7.35 us -> 3.17 us
    pallas_call x1 -> x0, local copies, waits for them, and re-layouts: 2.02 us -> none  [body(): pl.pallas_call(functools.partial(kernel, side, side, doms, cap, halo), ou...]
where the time goes in v2:
time: 125 us; the launch traced here: 123 us
  Pallas kernels  119 us (95%)
  local copies, waits for them, and re-layouts  3.17 us (3%)
    pallas_call x1, Pallas kernels, body(): pl.pallas_call(functools.partial(kernel, side, side, doms, cap, halo), ou...  119 us
    unnamed x2, local copies, waits for them, and re-layouts  3.17 us

profile of v2, /device:TPU:1, one launch (start us, length us, event | category | flops | bytes accessed | tf_op | source)
XLA Modules:
  0.0 123.0 jit_solution(8805194913096296580)
XLA Ops:
  0.6 119.2 %shard_map.176 = (bf16[227,1024]{1,0:T(8,128)(2,1)}, f32[48,128]{1,0:T(8,128)}) custom-call(bf16[474,1024]{1,0:T(8,128)(2,1)} %bitcast.13, bf16[256,512]{1,0:T(8,128)(2,1)} %refs_1_.1, bf16[2048,512]{1,0:T(8,128)(2,1)} %refs_2_.1, bf16[227,1024]{1,0:T(8,128)(2,1)} %bitcast.14, bf16[474,512]{1,0:T(8,128)(2,1)} %refs_4_.1, bf16[512,512]{1,0:T(8,128)(2,1)} %refs_5_.1, ...), custom_call_target="tpu_custom_call" | custom-call | flops 24999999488 | bytes 10000000 | tf_op jit(solution)/shard_map/pallas_call | solution.py:568
  119.8 1.8 %copy.21 = bf16[1024,227]{0,1:T(8,128)(2,1)} copy(bf16[1024,227]{0,1:T(8,128)(2,1)} %bitcast.12) | data formatting | bytes 929792
  121.7 1.3 %copy.22 = f32[48,128]{1,0:T(8,128)} copy(f32[48,128]{1,0:T(8,128)} %get-tuple-element.9) | data formatting | bytes 49152

commit v3 on v2

--- a/solution.py
+++ b/solution.py
@@ -11,7 +11,6 @@
 F32 = jnp.float32
 BF16 = jnp.bfloat16
 CHUNKS = 8
-EARLY = 2
 INPUTS = 17
 STRIDE = 53
 STRIDE_INVERSE = 29
@@ -127,8 +126,10 @@
         dsum,
         dpre,
         gland,
-        g2,
-        gl2,
+        line1,
+        land1,
+        line2,
+        land2,
         pick,
         a_send,
         a_recv,
@@ -140,11 +141,12 @@
         b_recv,
         p_send,
         p_recv,
+        q_send,
+        q_recv,
         g_send,
         g_recv,
     ) = refs
     n = nx * nz * 2 * ny
-    chips = nx * nz * ny
     width_in, grid = x_ref.shape
     nodes, width = ml_ref.shape
     edges = es_ref.shape[0]
@@ -255,11 +257,6 @@
 
     def encode(c, carry):
         take(rbuf.at[pl.ds(c * spc, spc)], a_recv.at[c])
-
-        @pl.when(c == CHUNKS - 1)
-        def _():
-            lax.fori_loop(0, EARLY, send_cot, 0)
-
         wide = unfold(rbuf[pl.ds(c * spc, spc)])
         mark = iota((rows, 128), 1) == width_in - (width - 128)
         label = jnp.sum(jnp.where(mark, wide[:, width - 128 :], 0.0), axis=1, keepdims=True)
@@ -320,7 +317,7 @@
 
     lax.fori_loop(0, CHUNKS, outbound, 0)
     pltpu.make_async_copy(obuf.at[0], inbuf.at[me], h_recv).start()
-    lax.fori_loop(EARLY, CHUNKS, send_cot, 0)
+    lax.fori_loop(0, CHUNKS, send_cot, 0)
 
     own_part = dot(enc[...], wedge_ref[2 * width :, :]).astype(BF16)
     mesh_part[...] = own_part
@@ -417,25 +414,52 @@
     lax.fori_loop(cut, nx * nz, send_pair, 0)
     take(gland, p_recv)
     cols = width // ny
+    third = share // 3
+    place3 = (lax.div(band, 2 * nz), lax.rem(lax.div(band, 2), nz), y)
 
     def add_pair(i, carry):
         block = pl.ds(pl.multiple_of((i * 2 + k) * share, 16), share)
         both = (hbuf[block, :].astype(F32) + gland[i].astype(F32)).astype(BF16)
+        tx, tz = lax.div(i, nz), lax.rem(i, nz)
         for d in range(ny):
-            g2[i * ny + d] = both[:, d * cols : (d + 1) * cols]
+            part3 = both[:, d * cols : (d + 1) * cols]
+            line1[0, tx, tz * ny + d] = part3[:third]
+            line1[1, tz, tx * ny + d] = part3[third : 2 * third]
+            line1[2, d, i] = part3[2 * third :]
         return carry
 
     lax.fori_loop(0, nx * nz, add_pair, 0)
-    chip = lax.div(band, 2) * ny + y
-
-    def send_grad(r, carry):
-        to = lax.rem(chip + r * STRIDE, chips)
-        xz = lax.div(to, ny)
-        send(g2.at[to], gl2.at[chip], g_send, g_recv, (xz * 2 + k, lax.rem(to, ny)))
-        return carry
-
-    lax.fori_loop(1, chips, send_grad, 0)
-    pltpu.make_async_copy(g2.at[chip], gl2.at[chip], g_recv).start()
+
+    def device(axis, along, rest):
+        two = [lax.div(rest, ny), lax.rem(rest, ny)]
+        tx, tz, ty = two[:axis] + [along] + two[axis:]
+        return (tx * nz + tz) * 2 + k, ty
+
+    def others(axis):
+        a, b = place3[:axis] + place3[axis + 1 :]
+        return a * ny + b
+
+    for step in range(1, ny):
+        for axis in range(3):
+            to = lax.rem(place3[axis] + step, ny)
+            send(
+                line1.at[axis, to], land1.at[axis, step - 1], q_send, q_recv.at[axis], device(axis, to, others(axis))
+            )
+    for axis in range(3):
+        take(land1.at[axis], q_recv.at[axis])
+        total = line1[axis, place3[axis]].astype(F32)
+        for step in range(1, ny):
+            total += land1[axis, step - 1].astype(F32)
+        line2[axis] = total.astype(BF16)
+        mine = others(axis)
+
+        def send_line(r, carry, axis=axis, mine=mine):
+            to = lax.rem(mine + r * 5, ny * ny)
+            send(line2.at[axis, to], land2.at[axis, mine], g_send, g_recv, device(axis, place3[axis], to))
+            return carry
+
+        lax.fori_loop(1, ny * ny, send_line, 0)
+        pltpu.make_async_copy(line2.at[axis, mine], land2.at[axis, mine], g_recv).start()
 
     take(bland, b_recv)
 
@@ -453,20 +477,21 @@
         return carry
 
     lax.fori_loop(0, grid // gpc, choose, 0)
-    take(gl2, g_recv)
-    grad_ref[...] = jnp.zeros_like(grad_ref)
-
-    def add_grad(i, carry):
-        grad_ref[...] += gl2[i].astype(F32)
-        return carry
-
-    lax.fori_loop(0, chips, add_grad, 0)
+    take(land2, g_recv)
+    for axis in range(3):
+        grad_ref[axis * third : (axis + 1) * third, :] = jnp.sum(land2[axis].astype(F32), axis=0)
     take(sbuf.at[pl.ds(1, n - 1)], a_send)
     take(csbuf.at[pl.ds(1, n - 1)], c_send)
     take(obuf.at[pl.ds(1, n - 1)], h_send)
     take(bsend.at[pl.ds(1, n - 1)], b_send)
     take(gland, p_send)
-    take(g2.at[pl.ds(1, chips - 1)], g_send)
+    take(land1, q_send)
+    take(land2.at[:, pl.ds(1, ny * ny - 1)], g_send)
+
+
+def hand_over(pred_ref, grad_ref, pred_out, grad_out):
+    pred_out[...] = pred_ref[...]
+    grad_out[...] = grad_ref[...]
 
 
 def body(
@@ -492,7 +517,6 @@
 ):
     side = int(round((bands // 2) ** 0.5))
     n = bands * doms
-    chips = n // 2
     grid = grid_inputs.shape[0]
     nodes, width = mesh_latent.shape
     edges = edge_state.shape[0]
@@ -537,14 +561,16 @@
         vmem((nodes, width), BF16),
         vmem((edges, width), BF16),
         vmem((bands // 2, share, width), BF16),
-        vmem((chips, share, cols), BF16),
-        vmem((chips, share, cols), BF16),
+        vmem((3, doms, doms * doms, share // 3, cols), BF16),
+        vmem((3, doms - 1, doms * doms, share // 3, cols), BF16),
+        vmem((3, doms * doms, share // 3, cols), BF16),
+        vmem((3, doms * doms, share // 3, cols), BF16),
         vmem((n * cap, grid), BF16),
     ]
     dma = pltpu.SemaphoreType.DMA
     for _ in range(2):
         scratch += [dma, dma((CHUNKS,))]
-    scratch += [dma] * 8
+    scratch += [dma] * 6 + [dma, dma((3,)), dma, dma]
     operands = (
         grid_inputs.T,
         mesh_latent,
@@ -579,6 +605,13 @@
         ),
         cost_estimate=pl.CostEstimate(flops=25 * 10**9, bytes_accessed=10**7, transcendentals=10**7),
     )(*operands)
+    results = (prediction, gradient)
+    prediction, gradient = pl.pallas_call(
+        hand_over,
+        out_shape=tuple(jax.ShapeDtypeStruct(a.shape, a.dtype) for a in results),
+        in_specs=[pl.BlockSpec(memory_space=vmem)] * 2,
+        out_specs=(pl.BlockSpec(memory_space=vmem),) * 2,
+    )(*results)
     return prediction.T, gradient
 
 

time: 125 us -> 120 us (0.960); the launches traced: 123 us -> 120 us
  local copies, waits for them, and re-layouts: 3.17 us -> 0 us
    unnamed x2 -> x0, local copies, waits for them, and re-layouts: 3.17 us -> none
    pallas_call x1, Pallas kernels: 119 us -> 117 us  [body(): pl.pallas_call(functools.partial(kernel, side, side, doms, cap, halo), ou...]
    pallas_call x0 -> x1, Pallas kernels: none -> 1.83 us  [body(): pl.pallas_call(hand_over, out_shape=tuple((jax.ShapeDtypeStruct(a.shape,...]
where the time goes in v3:
time: 120 us
  Pallas kernels  119 us (99%)
    pallas_call x1, Pallas kernels, body(): pl.pallas_call(functools.partial(kernel, side, side, doms, cap, halo), ou...  117 us

profile of v3, /device:TPU:1, one launch (start us, length us, event | category | flops | bytes accessed | tf_op | source)
XLA Modules:
  0.0 119.7 jit_solution(8160256802038544837)
XLA Ops:
  0.6 117.3 %shard_map.176 = (bf16[227,1024]{1,0:T(8,128)(2,1)}, f32[48,128]{1,0:T(8,128)}) custom-call(bf16[474,1024]{1,0:T(8,128)(2,1)} %bitcast.12, bf16[256,512]{1,0:T(8,128)(2,1)} %refs_1_.1, bf16[2048,512]{1,0:T(8,128)(2,1)} %refs_2_.1, bf16[227,1024]{1,0:T(8,128)(2,1)} %bitcast.13, bf16[474,512]{1,0:T(8,128)(2,1)} %refs_4_.1, bf16[512,512]{1,0:T(8,128)(2,1)} %refs_5_.1, ...), custom_call_target="tpu_custom_call" | custom-call | flops 24999999488 | bytes 10000000 | tf_op jit(solution)/shard_map/pallas_call | solution.py:594
  117.9 1.8 %shard_map.177 = (bf16[227,1024]{1,0:T(8,128)(2,1)}, f32[48,128]{1,0:T(8,128)}) custom-call(bf16[227,1024]{1,0:T(8,128)(2,1)} %get-tuple-element.6.pred_ref, f32[48,128]{1,0:T(8,128)} %get-tuple-element.7.grad_ref), custom_call_target="tpu_custom_call" | custom-call | tf_op jit(solution)/shard_map/pallas_call | solution.py:609

commit v4 on v3

--- a/solution.py
+++ b/solution.py
@@ -11,6 +11,7 @@
 F32 = jnp.float32
 BF16 = jnp.bfloat16
 CHUNKS = 8
+AHEAD = 4
 INPUTS = 17
 STRIDE = 53
 STRIDE_INVERSE = 29
@@ -204,8 +205,6 @@
     cs[first:, :] = jnp.zeros((cs.shape[0] - first, grid), BF16)
     cs[:outs, :] = cot_ref[...]
 
-    pl.semaphore_wait(barrier, n - 1)
-
     def send(src, dst, send_sem, recv_sem, to):
         pltpu.make_async_remote_copy(
             src_ref=src, dst_ref=dst, send_sem=send_sem, recv_sem=recv_sem, device_id=to, device_id_type=MESH
@@ -224,7 +223,7 @@
 
             return carry
 
-        lax.fori_loop(0, spc, one, 0)
+        lax.fori_loop(0, spc, one, 0, unroll=4)
 
         @pl.when(c == 0)
         def _():
@@ -234,11 +233,21 @@
         place = one_hot(slots[...] == iota((rows, grid), 0) + c * rows)
         pick[pl.ds(pl.multiple_of(c * rows, rows), rows), :] = place
         sbuf[pl.ds(c * spc, spc)] = fold(dot_t(place, xs[...]), spc, cap)
+        csbuf[pl.ds(c * spc, spc)] = fold(dot_t(place, cs[...]), spc, cap)
+        return carry
+
+    def pack_and_send(c, carry):
+        pack(c, carry)
+        return send_rows(c, carry)
+
+    def send_rows(c, carry):
         send_parts(c, sbuf, rbuf, a_send, a_recv, 1)
-        csbuf[pl.ds(c * spc, spc)] = fold(dot_t(place, cs[...]), spc, cap)
-        return carry
-
-    lax.fori_loop(0, CHUNKS, pack, 0)
+        return carry
+
+    lax.fori_loop(0, AHEAD, pack, 0)
+    pl.semaphore_wait(barrier, n - 1)
+    lax.fori_loop(0, AHEAD, send_rows, 0)
+    lax.fori_loop(AHEAD, CHUNKS, pack_and_send, 0)
 
     def send_cot(c, carry):
         send_parts(c, csbuf, crbuf, c_send, c_recv, 1)
@@ -312,7 +321,7 @@
 
             return inner
 
-        lax.fori_loop(0, spc, one, 0)
+        lax.fori_loop(0, spc, one, 0, unroll=4)
         return carry
 
     lax.fori_loop(0, CHUNKS, outbound, 0)
@@ -362,7 +371,7 @@
 
             return inner
 
-        lax.fori_loop(0, spc, one, 0)
+        lax.fori_loop(0, spc, one, 0, unroll=4)
         take(crbuf.at[pl.ds(c * spc, spc)], c_recv.at[c])
         slope = dot(unfold(crbuf[pl.ds(c * spc, spc)]).astype(BF16), wpt[...])
         slope = (slope * sig * (1.0 + zed * (1.0 - sig))).astype(BF16)

time: 120 us -> 119 us (level)
  no operation moved by 1% of the time
where the time goes in v4:
time: 119 us
  Pallas kernels  118 us (99%)
    pallas_call x1, Pallas kernels, body(): pl.pallas_call(functools.partial(kernel, side, side, doms, cap, halo), ou...  116 us

profile of v4, /device:TPU:1, one launch (start us, length us, event | category | flops | bytes accessed | tf_op | source)
XLA Modules:
  0.0 118.7 jit_solution(10784683808404886692)
XLA Ops:
  0.6 116.3 %shard_map.176 = (bf16[227,1024]{1,0:T(8,128)(2,1)}, f32[48,128]{1,0:T(8,128)}) custom-call(bf16[474,1024]{1,0:T(8,128)(2,1)} %bitcast.12, bf16[256,512]{1,0:T(8,128)(2,1)} %refs_1_.1, bf16[2048,512]{1,0:T(8,128)(2,1)} %refs_2_.1, bf16[227,1024]{1,0:T(8,128)(2,1)} %bitcast.13, bf16[474,512]{1,0:T(8,128)(2,1)} %refs_4_.1, bf16[512,512]{1,0:T(8,128)(2,1)} %refs_5_.1, ...), custom_call_target="tpu_custom_call" | custom-call | flops 24999999488 | bytes 10000000 | tf_op jit(solution)/shard_map/pallas_call | solution.py:603
  116.9 1.8 %shard_map.177 = (bf16[227,1024]{1,0:T(8,128)(2,1)}, f32[48,128]{1,0:T(8,128)}) custom-call(bf16[227,1024]{1,0:T(8,128)(2,1)} %get-tuple-element.6.pred_ref, f32[48,128]{1,0:T(8,128)} %get-tuple-element.7.grad_ref), custom_call_target="tpu_custom_call" | custom-call | tf_op jit(solution)/shard_map/pallas_call | solution.py:618

commit v5 on v4

--- a/solution.py
+++ b/solution.py
@@ -233,7 +233,6 @@
         place = one_hot(slots[...] == iota((rows, grid), 0) + c * rows)
         pick[pl.ds(pl.multiple_of(c * rows, rows), rows), :] = place
         sbuf[pl.ds(c * spc, spc)] = fold(dot_t(place, xs[...]), spc, cap)
-        csbuf[pl.ds(c * spc, spc)] = fold(dot_t(place, cs[...]), spc, cap)
         return carry
 
     def pack_and_send(c, carry):
@@ -248,6 +247,13 @@
     pl.semaphore_wait(barrier, n - 1)
     lax.fori_loop(0, AHEAD, send_rows, 0)
     lax.fori_loop(AHEAD, CHUNKS, pack_and_send, 0)
+
+    def pack_cot(c, carry):
+        place = pick[pl.ds(pl.multiple_of(c * rows, rows), rows), :]
+        csbuf[pl.ds(c * spc, spc)] = fold(dot_t(place, cs[...]), spc, cap)
+        return carry
+
+    lax.fori_loop(0, CHUNKS, pack_cot, 0)
 
     def send_cot(c, carry):
         send_parts(c, csbuf, crbuf, c_send, c_recv, 1)

time: 119 us -> 119 us (level)
  no operation moved by 1% of the time
where the time goes in v5:
time: 119 us; the launch traced here: 118 us
  Pallas kernels  117 us (98%)
    pallas_call x1, Pallas kernels, body(): pl.pallas_call(functools.partial(kernel, side, side, doms, cap, halo), ou...  115 us

profile of v5, /device:TPU:1, one launch (start us, length us, event | category | flops | bytes accessed | tf_op | source)
XLA Modules:
  0.0 118.0 jit_solution(14479451612567969780)
XLA Ops:
  0.6 115.5 %shard_map.176 = (bf16[227,1024]{1,0:T(8,128)(2,1)}, f32[48,128]{1,0:T(8,128)}) custom-call(bf16[474,1024]{1,0:T(8,128)(2,1)} %bitcast.12, bf16[256,512]{1,0:T(8,128)(2,1)} %refs_1_.1, bf16[2048,512]{1,0:T(8,128)(2,1)} %refs_2_.1, bf16[227,1024]{1,0:T(8,128)(2,1)} %bitcast.13, bf16[474,512]{1,0:T(8,128)(2,1)} %refs_4_.1, bf16[512,512]{1,0:T(8,128)(2,1)} %refs_5_.1, ...), custom_call_target="tpu_custom_call" | custom-call | flops 24999999488 | bytes 10000000 | tf_op jit(solution)/shard_map/pallas_call | solution.py:609
  116.1 1.8 %shard_map.177 = (bf16[227,1024]{1,0:T(8,128)(2,1)}, f32[48,128]{1,0:T(8,128)}) custom-call(bf16[227,1024]{1,0:T(8,128)(2,1)} %get-tuple-element.6.pred_ref, f32[48,128]{1,0:T(8,128)} %get-tuple-element.7.grad_ref), custom_call_target="tpu_custom_call" | custom-call | tf_op jit(solution)/shard_map/pallas_call | solution.py:624
